TPU v7x, 32 devices: a whole 2x2x4 slice. The times are simulated.
32 devices in a mesh: mp: 8 (over z, x), dp: 4 (over y, core).
Axes of the slice: x: 2, y: 2, z: 4, core: 2. Of those that a mesh axis runs over, the one named last changes fastest.
Arguments:
- pre_act: bfloat16 [512, 36864], P('dp', 'mp'), may hold values from -5 to 5
- cotangent: bfloat16 [512, 10240], P('mp', 'dp'), may hold values from -6 to 6
- down_weight: bfloat16 [36864, 10240], P('mp', 'dp'), may hold values from -0.03125 to 0.03125
- first_moment: bfloat16 [36864, 10240], P('mp', 'dp'), may hold values from -4.0625 to 4.0625
- second_moment: bfloat16 [36864, 10240], P('mp', 'dp'), may hold values from 1.0234375 to 51
Outputs:
- input_grad: bfloat16 [512, 36864], P('dp', 'mp')
- step_update: bfloat16 [36864, 10240], P('mp', 'dp')
All inputs are finite; a program needn't handle non-finite values.
Results may differ from a plain program's by a relative error of at most 0.023.
Values may be sent and summed in bfloat16 or wider, within the bound.
A program may use at most 192 MiB of HBM per device.

v0:
```python
import jax
import jax.numpy as jnp
from jax import lax
from jax.sharding import PartitionSpec as P

STEP = 20


gelu_scale = 0.7978845608028654
gelu_cubic = 0.044715
beta_one = 0.9
beta_two = 0.95
epsilon = 1e-08


def gelu_parts(values):
    tangent = jnp.tanh(gelu_scale * (values + gelu_cubic * values * values * values))
    output = 0.5 * values * (1.0 + tangent)
    slopes = 0.5 * (1.0 + tangent) + 0.5 * values * (1.0 - tangent * tangent) * gelu_scale * (
        1.0 + 3.0 * gelu_cubic * values * values
    )
    return (output, slopes)


def adam_update(gradient, first_moment, second_moment):
    moment_one = beta_one * first_moment.astype(jnp.float32) + (1.0 - beta_one) * gradient
    moment_two = (
        beta_two * second_moment.astype(jnp.float32) + (1.0 - beta_two) * gradient * gradient
    )
    corrected = moment_one / (1.0 - beta_one**STEP)
    scaled = jnp.sqrt(moment_two / (1.0 - beta_two**STEP))
    return (corrected / (scaled + epsilon)).astype(jnp.bfloat16)


def shards(pre_act, cotangent, down_weight, first_moment, second_moment):
    contract_rows = (((0,), (0,)), ((), ()))
    contract_cols = (((1,), (1,)), ((), ()))
    cot_whole = lax.all_gather(cotangent, "mp", axis=0, tiled=True)
    pre_whole = lax.all_gather(pre_act, "dp", axis=0, tiled=True)
    output, unused = gelu_parts(pre_whole.astype(jnp.float32))
    gradient = lax.dot_general(
        output.astype(jnp.bfloat16), cot_whole, contract_rows, preferred_element_type=jnp.float32
    )
    step_update = adam_update(gradient, first_moment, second_moment)
    hidden_grad = lax.psum_scatter(
        lax.dot_general(
            cot_whole, down_weight, contract_cols, preferred_element_type=jnp.float32
        ).astype(jnp.bfloat16),
        "dp",
        scatter_dimension=0,
        tiled=True,
    ).astype(jnp.float32)
    unused, slopes = gelu_parts(pre_act.astype(jnp.float32))
    input_grad = (hidden_grad * slopes).astype(jnp.bfloat16)
    return (input_grad, step_update)


def solution(mesh):
    placed = (P("dp", "mp"), P("mp", "dp"), P("mp", "dp"), P("mp", "dp"), P("mp", "dp"))
    return jax.shard_map(
        shards,
        mesh=mesh,
        in_specs=placed,
        out_specs=(P("dp", "mp"), P("mp", "dp")),
        check_vma=False,
    )
```

profile of v0, /device:TPU:0, one launch (start us, length us, event | category | flops | bytes accessed | tf_op | source)
XLA Modules:
  0.0 169.7 jit_solution(7793024930163945561)
XLA Ops:
  7.2 0.0 all-gather.3.cloned.1.call-start
  7.2 0.7 all-gather.3.cloned.1.call-update
  7.9 0.0 all-gather.5.cloned.1.call-start
  7.9 0.7 all-gather.5.cloned.1.call-update
  8.6 0.0 reduce-scatter.2.cloned.1.call-start
  8.7 58.9 %all-gather.3.cloned.1.call-done = bf16[512,2560]{1,0:T(8,128)(2,1)} async-done(((bf16[64,2560]{1,0:T(8,128)(2,1)}), bf16[512,2560]{1,0:T(8,128)(2,1)}) %all-gather.3.cloned.1.call-update) | async-done | bytes 2621456 | tf_op jit(solution)/shard_map/all_gather | solution.py:38
  67.6 19.2 %convolution_convert_fusion = bf16[512,4608]{1,0:T(8,128)(2,1)} fusion(bf16[512,2560]{1,0:T(8,128)(2,1)} %all-gather.3.cloned.1.call-done, bf16[4608,2560]{1,0:T(8,128)(2,1)} %param.7), kind=kOutput, calls=%fused_computation.17 | convolution fusion | flops 12081954816 | bytes 30932992 | tf_op jit(solution)/shard_map/dot_general | solution.py:46
  86.7 0.0 reduce-scatter.2.cloned.1.call-update
  86.8 0.0 copy-start
  86.8 18.4 %all-gather.5.cloned.1.call-done = bf16[512,4608]{1,0:T(8,128)(2,1)} async-done(((bf16[128,4608]{1,0:T(8,128)(2,1)}), bf16[512,4608]{1,0:T(8,128)(2,1)}) %all-gather.5.cloned.1.call-update) | async-done | bytes 4718608 | tf_op jit(solution)/shard_map/all_gather | solution.py:39
  105.2 54.1 %fusion.5 = bf16[4608,2560]{1,0:T(8,128)(2,1)} fusion(bf16[4608,2560]{1,0:T(8,128)(2,1)} %param.9, bf16[4608,2560]{1,0:T(8,128)(2,1)} %param.8, bf16[512,2560]{1,0:T(8,128)(2,1)} %all-gather.3.cloned.1.call-done, bf16[512,4608]{1,0:T(8,128)(2,1)} %all-gather.5.cloned.1.call-done), kind=kOutput, calls=%fused_computation.6 | convolution fusion | flops 12268339200 | bytes 78118912 | tf_op jit(solution)/shard_map/dot_general | solution.py:41
  159.3 0.0 reduce-scatter.2.cloned.1.call-done
  159.3 0.0 copy-done
  159.3 3.9 %fusion.23 = bf16[128,4608]{1,0:T(8,128)(2,1)} fusion(bf16[128,4608]{1,0:T(8,128)(2,1)S(1)} %copy-done, bf16[128,4608]{1,0:T(8,128)(2,1)} %reduce-scatter.2.cloned.1.call-done), kind=kLoop, calls=%fused_computation.36 | loop fusion | flops 12386304 | bytes 3538944 | tf_op jit(solution)/shard_map/convert_element_type | solution.py:54
Async XLA Ops:
  7.2 60.4 %all-gather.3.cloned.1.call-start = ((), (), s32[]{:S(2)}) async-start(), calls=%async_computation.1 | async-start | bytes 2949120 | tf_op jit(solution)/shard_map/all_gather | solution.py:38
  7.9 97.3 %all-gather.5.cloned.1.call-start = ((), (), s32[]{:S(2)}) async-start(), calls=%async_computation.3 | async-start | bytes 5898240 | tf_op jit(solution)/shard_map/all_gather | solution.py:39
  8.6 150.6 %reduce-scatter.2.cloned.1.call-start = ((), (), s32[]{:S(2)}) async-start(), calls=%async_computation.2 | async-start | bytes 5898240 | tf_op jit(solution)/shard_map/reduce_scatter | solution.py:45
  86.8 72.5 %copy-start = (bf16[128,4608]{1,0:T(8,128)(2,1)S(1)}, bf16[128,4608]{1,0:T(8,128)(2,1)}, u32[]{:S(2)}) copy-start(bf16[128,4608]{1,0:T(8,128)(2,1)} %param.5) | copy-start | bytes 3538948
Sparse Core Ops, SparseCore 0:
  10.2 57.3 all-gather.2
  69.1 36.0 all-gather.4
  107.7 47.8 reduce-scatter.1
where the time goes:
time: 170 us
  waiting for transfers between devices  78.7 us (46%)
  matrix products  73.2 us (43%)
  between operations  13.8 us (8%)
  other arithmetic  3.92 us (2%)
    all_gather x1, waiting for transfers between devices, shards(): cot_whole = lax.all_gather(cotangent, 'mp', axis=0, tiled=True)  58.9 us
    dot_general x1, matrix products, shards(): lax.dot_general(output.astype(jnp.bfloat16), cot_whole, contract_rows, pr...  54.1 us
    dot_general x1, matrix products, shards(): lax.dot_general(cot_whole, down_weight, contract_cols, preferred_element_...  19.2 us
    all_gather x1, waiting for transfers between devices, shards(): pre_whole = lax.all_gather(pre_act, 'dp', axis=0, tiled=True)  18.4 us
    convert_element_type x1, other arithmetic, shards(): input_grad = (hidden_grad * slopes).astype(jnp.bfloat16)  3.92 us
  transfers between devices with their start and end apart: 3, of which 2 were waited for; matrix products, arithmetic and copies ran while one was open for 43% of the time, Pallas kernels for 0%

commit v1 on v0

v1 whole, which is shorter than its diff:
```python
import functools

import jax
import jax.numpy as jnp
from jax import lax
from jax.experimental import pallas as pl
from jax.experimental.pallas import tpu as pltpu
from jax.sharding import PartitionSpec as P

STEP = 20

MESH = pl.DeviceIdType.MESH

gelu_scale = 0.7978845608028654
gelu_cubic = 0.044715
beta_one = 0.9
beta_two = 0.95
epsilon = 1e-08


def gelu_output(values):
    tangent = jnp.tanh(gelu_scale * (values + gelu_cubic * values * values * values))
    return 0.5 * values * (1.0 + tangent)


def gelu_slopes(values):
    tangent = jnp.tanh(gelu_scale * (values + gelu_cubic * values * values * values))
    return 0.5 * (1.0 + tangent) + 0.5 * values * (1.0 - tangent * tangent) * gelu_scale * (
        1.0 + 3.0 * gelu_cubic * values * values
    )


def adam_step(gradient, first, second):
    gain = (1.0 - beta_one) / (1.0 - beta_one**STEP)
    spread = 1.0 / ((1.0 - beta_two**STEP) * gain * gain)
    moment_one = (beta_one / (1.0 - beta_one)) * first + gradient
    moment_two = (beta_two * spread) * second + ((1.0 - beta_two) * spread) * (gradient * gradient)
    scaled = moment_two * lax.rsqrt(moment_two)
    return moment_one * pl.reciprocal(scaled + epsilon / gain, approx=True)


def exchange_kernel(
    chunks, pieces, block,
    pre_ref, cot_ref, weight_ref,
    cot_all, hid_all, mine_ref, away_ref,
    weight, hidden, total, part, other,
    weight_sem, own_sem, ring_send, ring_recv, hid_send, hid_recv, fwd_send, fwd_recv,
    pair_send, pair_recv,
):
    mp, dp = lax.axis_index("mp"), lax.axis_index("dp")
    tokens, features = cot_ref.shape
    units = weight_ref.shape[0]
    wide = features // chunks
    tall = units // pieces
    rows = pre_ref.shape[0]

    x, z = mp % 2, mp // 2
    place = z + x * (7 - 2 * z)

    def index_of(position):
        p = (position + 16) % 8
        side = p // 4
        return 2 * (p + side * (7 - 2 * p)) + side

    ring = (index_of(place + 1), index_of(place - 1))
    core, y = dp % 2, dp // 2
    sibling = 2 * y + (1 - core)
    across = 2 * (1 - y) + core

    def columns(k):
        return pl.ds(k * wide, wide)

    loads = []
    for k in range(chunks):
        load = pltpu.make_async_copy(
            weight_ref.at[:, columns(k)], weight.at[:, columns(k)], weight_sem.at[k]
        )
        load.start()
        loads.append(load)

    barrier = pltpu.get_barrier_semaphore()
    for position in ring:
        pl.semaphore_signal(barrier, inc=1, device_id={"mp": position}, device_id_type=MESH)
    for position in (sibling, across):
        pl.semaphore_signal(barrier, inc=1, device_id={"dp": position}, device_id_type=MESH)
    cot_all[mp] = cot_ref[...]
    pl.semaphore_wait(barrier, 4)

    def hops(k, way):
        return 4 if k % 2 == way else 3

    def ring_copy(k, hop, way):
        origin = index_of(place - hop if way == 0 else place + hop)
        return pltpu.make_async_remote_copy(
            src_ref=cot_all.at[origin, :, columns(k)],
            dst_ref=cot_all.at[origin, :, columns(k)],
            send_sem=ring_send.at[k, hop, way],
            recv_sem=ring_recv.at[k, hop, way],
            device_id={"mp": ring[way]},
            device_id_type=MESH,
        )

    def ring_wait(k, hop, way):
        origin = index_of(place - hop - 1 if way == 0 else place + hop + 1)
        pltpu.make_async_remote_copy(
            src_ref=cot_all.at[origin, :, columns(k)],
            dst_ref=cot_all.at[origin, :, columns(k)],
            send_sem=ring_send.at[k, hop, way],
            recv_sem=ring_recv.at[k, hop, way],
            device_id={"mp": ring[way]},
            device_id_type=MESH,
        ).wait_recv()

    def hid_rows(j):
        return pl.ds(j * tall, tall)

    def hid_copy(j, which):
        return pltpu.make_async_remote_copy(
            src_ref=hidden.at[hid_rows(j), :],
            dst_ref=hid_all.at[dp, hid_rows(j), :],
            send_sem=hid_send.at[j, which],
            recv_sem=hid_recv.at[j, which],
            device_id={"dp": (across, sibling)[which]},
            device_id_type=MESH,
        )

    def hid_wait(j, which):
        origin = (across, sibling)[which]
        pltpu.make_async_remote_copy(
            src_ref=hidden.at[hid_rows(j), :],
            dst_ref=hid_all.at[origin, hid_rows(j), :],
            send_sem=hid_send.at[j, which],
            recv_sem=hid_recv.at[j, which],
            device_id={"dp": origin},
            device_id_type=MESH,
        ).wait_recv()

    def forward_copy(j, origin):
        return pltpu.make_async_remote_copy(
            src_ref=hid_all.at[origin, hid_rows(j), :],
            dst_ref=hid_all.at[origin, hid_rows(j), :],
            send_sem=fwd_send.at[j],
            recv_sem=fwd_recv.at[j],
            device_id={"dp": sibling},
            device_id_type=MESH,
        )

    sent = []
    kept = []
    for k in range(chunks):
        for way in (0, 1):
            copy = ring_copy(k, 0, way)
            copy.start()
            sent.append(copy)

    for j in range(pieces):
        values = pre_ref[:, j * tall : (j + 1) * tall].astype(jnp.float32)
        hidden[hid_rows(j), :] = gelu_output(values).T.astype(jnp.bfloat16)
        for which in (0, 1):
            copy = hid_copy(j, which)
            copy.start()
            sent.append(copy)
        copy = pltpu.make_async_copy(
            hidden.at[hid_rows(j), :], hid_all.at[dp, hid_rows(j), :], own_sem.at[j]
        )
        copy.start()
        kept.append(copy)

    def multiply(k, first, last):
        loads[k].wait()
        cot = cot_all[:, :, k * wide : (k + 1) * wide].reshape(8 * tokens, wide)

        def one(i, carry):
            at = pl.ds(pl.multiple_of(i * block, block), block)
            product = lax.dot_general(
                cot,
                weight[at, columns(k)],
                (((1,), (1,)), ((), ())),
                preferred_element_type=jnp.float32,
            )
            if not first:
                product = product + total[:, at]
            if not last:
                total[:, at] = product
                return carry
            part[:, :, at] = product.astype(jnp.bfloat16).reshape(4, rows, block)
            for side in (0, 1):
                pair_copy(i, side).start()
            return carry

        lax.fori_loop(0, units // block, one, 0)

    def pair_copy(i, side):
        at = pl.ds(pl.multiple_of(i * block, block), block)
        return pltpu.make_async_remote_copy(
            src_ref=part.at[2 * side + 1 - core, :, at],
            dst_ref=other.at[side, :, at],
            send_sem=pair_send.at[i, side],
            recv_sem=pair_recv.at[i, side],
            device_id={"dp": sibling},
            device_id_type=MESH,
        )

    for step in range(chunks + 3):
        done = None
        for k in range(chunks):
            hop = step - k
            if hop < 0 or hop > 3:
                continue
            for way in (0, 1):
                if hop < hops(k, way):
                    ring_wait(k, hop, way)
                    if hop + 1 < hops(k, way):
                        copy = ring_copy(k, hop + 1, way)
                        copy.start()
                        sent.append(copy)
            if hop == 3:
                done = k
        if 0 <= step - 2 < pieces:
            hid_wait(step - 2, 0)
            copy = forward_copy(step - 2, across)
            copy.start()
            sent.append(copy)
        if done is not None:
            multiply(done, done == 0, done == chunks - 1)

    def combine(i, carry):
        at = pl.ds(pl.multiple_of(i * block, block), block)
        for side in (0, 1):
            pair_copy(i, side).wait()
        mine = part[2 * y + core, :, at].astype(jnp.float32) + other[y, :, at].astype(jnp.float32)
        away = part[2 * (1 - y) + core, :, at].astype(jnp.float32) + other[1 - y, :, at].astype(
            jnp.float32
        )
        mine_ref[:, at] = mine.astype(jnp.bfloat16)
        away_ref[:, at] = away.astype(jnp.bfloat16)
        return carry

    lax.fori_loop(0, units // block, combine, 0)

    for j in range(pieces):
        hid_wait(j, 1)
        forward_copy(j, 2 * (1 - y) + (1 - core)).wait_recv()
    for copy in sent:
        copy.wait_send()
    for copy in kept:
        copy.wait()


def exchange(pre_act, cotangent, weight):
    rows, units = pre_act.shape
    tokens, features = cotangent.shape
    chunks, pieces, block = 5, 6, 512
    vmem = pl.BlockSpec(memory_space=pltpu.VMEM)
    hbm = pl.BlockSpec(memory_space=pl.ANY)
    bf16 = jnp.bfloat16
    dma = pltpu.SemaphoreType.DMA
    return pl.pallas_call(
        functools.partial(exchange_kernel, chunks, pieces, block),
        out_shape=(
            jax.ShapeDtypeStruct((8, tokens, features), bf16),
            jax.ShapeDtypeStruct((4, units, rows), bf16),
            jax.ShapeDtypeStruct((rows, units), bf16),
            jax.ShapeDtypeStruct((rows, units), bf16),
        ),
        in_specs=[vmem, vmem, hbm],
        out_specs=(vmem, hbm, vmem, vmem),
        scratch_shapes=[
            pltpu.VMEM((units, features), bf16),
            pltpu.VMEM((units, rows), bf16),
            pltpu.VMEM((8 * tokens, units), jnp.float32),
            pltpu.VMEM((4, rows, units), bf16),
            pltpu.VMEM((2, rows, units), bf16),
            dma((chunks,)),
            dma((pieces,)),
            dma((chunks, 4, 2)),
            dma((chunks, 4, 2)),
            dma((pieces, 2)),
            dma((pieces, 2)),
            dma((pieces,)),
            dma((pieces,)),
            dma((units // block, 2)),
            dma((units // block, 2)),
        ],
        compiler_params=pltpu.CompilerParams(
            collective_id=0, has_side_effects=True, vmem_limit_bytes=60 * 2**20
        ),
        name="exchange",
    )(pre_act, cotangent, weight)


def update_kernel(tile, hid_ref, cot_ref, first_ref, second_ref, out_ref):
    hidden = jnp.concatenate([hid_ref[i] for i in range(hid_ref.shape[0])], axis=1)
    for start in range(0, out_ref.shape[1], tile):
        at = slice(start, start + tile)
        gradient = jnp.dot(hidden, cot_ref[:, at], preferred_element_type=jnp.float32)
        out_ref[:, at] = adam_step(
            gradient, first_ref[:, at].astype(jnp.float32), second_ref[:, at].astype(jnp.float32)
        ).astype(jnp.bfloat16)


def update(hid_all, cot_whole, first_moment, second_moment):
    units, features = first_moment.shape
    groups, _, rows = hid_all.shape
    tall = 256
    block = pl.BlockSpec((tall, features), lambda i: (i, 0))
    return pl.pallas_call(
        functools.partial(update_kernel, 512 if features % 512 == 0 else 128),
        out_shape=jax.ShapeDtypeStruct((units, features), jnp.bfloat16),
        grid=(units // tall,),
        in_specs=[
            pl.BlockSpec((groups, tall, rows), lambda i: (0, i, 0)),
            pl.BlockSpec(cot_whole.shape, lambda i: (0, 0)),
            block,
            block,
        ],
        out_specs=block,
        compiler_params=pltpu.CompilerParams(vmem_limit_bytes=56 * 2**20),
        cost_estimate=pl.CostEstimate(
            flops=2 * groups * rows * units * features,
            bytes_accessed=6 * units * features,
            transcendentals=2 * units * features,
        ),
        name="update",
    )(hid_all, cot_whole, first_moment, second_moment)


def shards(pre_act, cotangent, down_weight, first_moment, second_moment):
    cot_all, hid_all, mine, away = exchange(pre_act, cotangent, down_weight)
    arrived = lax.ppermute(away, "dp", [(0, 2), (1, 3), (2, 0), (3, 1)])
    cot_whole = cot_all.reshape(-1, cot_all.shape[-1])
    step_update = update(hid_all, cot_whole, first_moment, second_moment)
    hidden_grad = mine.astype(jnp.float32) + arrived.astype(jnp.float32)
    input_grad = (hidden_grad * gelu_slopes(pre_act.astype(jnp.float32))).astype(jnp.bfloat16)
    return (input_grad, step_update)


def shards_any(pre_act, cotangent, down_weight, first_moment, second_moment):
    cot_whole = lax.all_gather(cotangent, "mp", axis=0, tiled=True)
    hidden = gelu_output(pre_act.astype(jnp.float32)).astype(jnp.bfloat16)
    hid_all = lax.all_gather(hidden.T, "dp", axis=0)
    partial_sum = lax.dot_general(
        cot_whole, down_weight, (((1,), (1,)), ((), ())), preferred_element_type=jnp.float32
    ).astype(jnp.bfloat16)
    hidden_grad = lax.psum_scatter(
        partial_sum, "dp", scatter_dimension=0, tiled=True
    ).astype(jnp.float32)
    step_update = update(hid_all, cot_whole, first_moment, second_moment)
    input_grad = (hidden_grad * gelu_slopes(pre_act.astype(jnp.float32))).astype(jnp.bfloat16)
    return (input_grad, step_update)


def solution(mesh):
    placed = (P("dp", "mp"), P("mp", "dp"), P("mp", "dp"), P("mp", "dp"), P("mp", "dp"))
    small = mesh.shape["mp"] == 8 and mesh.shape["dp"] == 4
    return jax.shard_map(
        shards if small else shards_any,
        mesh=mesh,
        in_specs=placed,
        out_specs=(P("dp", "mp"), P("mp", "dp")),
        check_vma=False,
    )
```

time: 170 us -> 95.4 us (0.56)
  Pallas kernels: 0 us -> 90.1 us
  waiting for transfers between devices: 78.7 us -> 0.01 us
  matrix products: 73.2 us -> 0 us
  between operations: 13.8 us -> 0.65 us
    pallas_call x0 -> x2, Pallas kernels: none -> 90.1 us  [the longest x1 52.5 us: exchange(): pl.pallas_call(functools.partial(exchange_kernel, chunks, pieces, block),...]
    all_gather x2 -> x0, waiting for transfers between devices: 77.3 us -> none  [the longest x1 58.9 us: shards(): cot_whole = lax.all_gather(cotangent, 'mp', axis=0, tiled=True)]
    dot_general x2 -> x0, matrix products: 73.2 us -> none  [the longest x1 54.1 us: shards(): lax.dot_general(output.astype(jnp.bfloat16), cot_whole, contract_rows, pr...]
  transfers between devices with their start and end apart: 3 -> 1, of which waited for: 2 -> 0; matrix products, arithmetic and copies ran while one was open for 43% -> 0% of each run, Pallas kernels for 0% -> 40%
where the time goes in v1:
time: 95.4 us; the launch traced here: 94.7 us
  Pallas kernels  90.1 us (94%)
  other arithmetic  2.8 us (3%)
  starting transfers between devices  1.1 us (1%)
    pallas_call x1, Pallas kernels, exchange(): pl.pallas_call(functools.partial(exchange_kernel, chunks, pieces, block),...  52.5 us
    pallas_call x1, Pallas kernels, update(): pl.pallas_call(functools.partial(update_kernel, 512 if features % 512 ==...  37.7 us
    convert_element_type x1, other arithmetic, shards(): (hidden_grad * gelu_slopes(pre_act.astype(jnp.float32))).astype(jnp.bfloa...  2.8 us
  transfers between devices with their start and end apart: 1, of which 0 were waited for; matrix products, arithmetic and copies ran while one was open for 0% of the time, Pallas kernels for 40%

profile of v1, /device:TPU:0, one launch (start us, length us, event | category | flops | bytes accessed | tf_op | source)
XLA Modules:
  0.0 94.7 jit_solution(14519256326989309911)
XLA Ops:
  0.6 52.5 %exchange.1 = (bf16[8,64,2560]{2,1,0:T(8,128)(2,1)}, bf16[4,4608,128]{2,1,0:T(8,128)(2,1)}, bf16[128,4608]{1,0:T(8,128)(2,1)}, bf16[128,4608]{1,0:T(8,128)(2,1)}) custom-call(bf16[128,4608]{1,0:T(8,128)(2,1)} %pre_ref.1, bf16[64,2560]{1,0:T(8,128)(2,1)} %cot_ref.1, bf16[4608,2560]{1,0:T(8,128)(2,1)} %weight_ref.1), custom_call_target="tpu_custom_call" | custom-call | tf_op jit(solution)/shard_map/exchange/pallas_call | solution.py:258
  53.1 1.1 %collective-permute-start = (bf16[128,4608]{1,0:T(8,128)(2,1)}, bf16[128,4608]{1,0:T(8,128)(2,1)S(1)}, u32[]{:S(2)}, u32[]{:S(2)}) collective-permute-start(bf16[128,4608]{1,0:T(8,128)(2,1)} %get-tuple-element.7), channel_id=1, source_target_pairs={{0,2},{1,3},{2,0},{3,1},{4,6},{5,7},{6,4},{7,5},{8,10},{9,11},{10,... | collective-permute-start | bytes 3538952 | tf_op jit(solution)/shard_map/ppermute | solution.py:330
  54.2 0.0 copy-start
  54.2 0.0 copy-start.1
  54.2 37.7 %update.1 = bf16[4608,2560]{1,0:T(8,128)(2,1)} custom-call(bf16[4,4608,128]{2,1,0:T(8,128)(2,1)} %get-tuple-element.8.hid_ref, bf16[512,2560]{1,0:T(8,128)(2,1)} %bitcast.1, bf16[4608,2560]{1,0:T(8,128)(2,1)} %first_ref.1, bf16[4608,2560]{1,0:T(8,128)(2,1)} %second_ref.1), custom_call_target="tpu_custom_call" | custom-call | flops 12079595520 | bytes 70778880 | tf_op jit(solution)/shard_map/update/pallas_call | solution.py:307
  91.9 0.0 collective-permute-done
  91.9 0.0 copy-done
  91.9 0.0 copy-done.1
  91.9 2.8 %fusion.7 = bf16[128,4608]{1,0:T(8,128)(2,1)} fusion(bf16[128,4608]{1,0:T(8,128)(2,1)S(1)} %copy-done, bf16[128,4608]{1,0:T(8,128)(2,1)S(1)} %collective-permute-done, bf16[128,4608]{1,0:T(8,128)(2,1)S(1)} %copy-done.1), kind=kLoop, calls=%fused_computation.14 | loop fusion | flops 13565952 | bytes 4718592 | tf_op jit(solution)/shard_map/convert_element_type | solution.py:334
Async XLA Ops:
  53.1 38.8 %collective-permute-start = (bf16[128,4608]{1,0:T(8,128)(2,1)}, bf16[128,4608]{1,0:T(8,128)(2,1)S(1)}, u32[]{:S(2)}, u32[]{:S(2)}) collective-permute-start(bf16[128,4608]{1,0:T(8,128)(2,1)} %get-tuple-element.7), channel_id=1, source_target_pairs={{0,2},{1,3},{2,0},{3,1},{4,6},{5,7},{6,4},{7,5},{8,10},{9,11},{10,... | collective-permute-start | bytes 3538952 | tf_op jit(solution)/shard_map/ppermute | solution.py:330
  54.2 37.7 %copy-start = (bf16[128,4608]{1,0:T(8,128)(2,1)S(1)}, bf16[128,4608]{1,0:T(8,128)(2,1)}, u32[]{:S(2)}) copy-start(bf16[128,4608]{1,0:T(8,128)(2,1)} %pre_ref.1) | copy-start | bytes 3538948
  54.2 37.7 %copy-start.1 = (bf16[128,4608]{1,0:T(8,128)(2,1)S(1)}, bf16[128,4608]{1,0:T(8,128)(2,1)}, u32[]{:S(2)}) copy-start(bf16[128,4608]{1,0:T(8,128)(2,1)} %get-tuple-element.6) | copy-start | bytes 3538948

commit v2 on v1

--- a/solution.py
+++ b/solution.py
@@ -31,12 +31,13 @@
 
 
 def adam_step(gradient, first, second):
-    gain = (1.0 - beta_one) / (1.0 - beta_one**STEP)
-    spread = 1.0 / ((1.0 - beta_two**STEP) * gain * gain)
-    moment_one = (beta_one / (1.0 - beta_one)) * first + gradient
-    moment_two = (beta_two * spread) * second + ((1.0 - beta_two) * spread) * (gradient * gradient)
-    scaled = moment_two * lax.rsqrt(moment_two)
-    return moment_one * pl.reciprocal(scaled + epsilon / gain, approx=True)
+    root = ((1.0 - beta_two) / (1.0 - beta_two**STEP)) ** 0.5
+    gain = (1.0 - beta_one) / (1.0 - beta_one**STEP) / root
+    kind = gradient.dtype
+    moment_one = kind.type(beta_one / (1.0 - beta_one)) * first + gradient
+    moment_two = kind.type(beta_two / (1.0 - beta_two)) * second + gradient * gradient
+    scaled = moment_two * lax.rsqrt(moment_two) + kind.type(epsilon / root)
+    return kind.type(gain) * moment_one * pl.reciprocal(scaled, approx=True)
 
 
 def exchange_kernel(
@@ -147,13 +148,13 @@
 
     sent = []
     kept = []
-    for k in range(chunks):
+    def ring_begin(k):
         for way in (0, 1):
             copy = ring_copy(k, 0, way)
             copy.start()
             sent.append(copy)
 
-    for j in range(pieces):
+    def hid_begin(j):
         values = pre_ref[:, j * tall : (j + 1) * tall].astype(jnp.float32)
         hidden[hid_rows(j), :] = gelu_output(values).T.astype(jnp.bfloat16)
         for which in (0, 1):
@@ -166,12 +167,18 @@
         copy.start()
         kept.append(copy)
 
+    for ahead in (0, 1):
+        ring_begin(ahead)
+        hid_begin(ahead)
+
     def multiply(k, first, last):
         loads[k].wait()
         cot = cot_all[:, :, k * wide : (k + 1) * wide].reshape(8 * tokens, wide)
 
+        span = block if last else 2 * block
+
         def one(i, carry):
-            at = pl.ds(pl.multiple_of(i * block, block), block)
+            at = pl.ds(pl.multiple_of(i * span, span), span)
             product = lax.dot_general(
                 cot,
                 weight[at, columns(k)],
@@ -188,7 +195,7 @@
                 pair_copy(i, side).start()
             return carry
 
-        lax.fori_loop(0, units // block, one, 0)
+        lax.fori_loop(0, units // span, one, 0)
 
     def pair_copy(i, side):
         at = pl.ds(pl.multiple_of(i * block, block), block)
@@ -216,6 +223,10 @@
                         sent.append(copy)
             if hop == 3:
                 done = k
+        if step + 2 < chunks:
+            ring_begin(step + 2)
+        if step + 2 < pieces:
+            hid_begin(step + 2)
         if 0 <= step - 2 < pieces:
             hid_wait(step - 2, 0)
             copy = forward_copy(step - 2, across)
@@ -250,7 +261,7 @@
 def exchange(pre_act, cotangent, weight):
     rows, units = pre_act.shape
     tokens, features = cotangent.shape
-    chunks, pieces, block = 5, 6, 512
+    chunks, pieces, block = 5, 6, 768
     vmem = pl.BlockSpec(memory_space=pltpu.VMEM)
     hbm = pl.BlockSpec(memory_space=pl.ANY)
     bf16 = jnp.bfloat16
@@ -291,18 +302,25 @@
 
 def update_kernel(tile, hid_ref, cot_ref, first_ref, second_ref, out_ref):
     hidden = jnp.concatenate([hid_ref[i] for i in range(hid_ref.shape[0])], axis=1)
-    for start in range(0, out_ref.shape[1], tile):
-        at = slice(start, start + tile)
-        gradient = jnp.dot(hidden, cot_ref[:, at], preferred_element_type=jnp.float32)
-        out_ref[:, at] = adam_step(
-            gradient, first_ref[:, at].astype(jnp.float32), second_ref[:, at].astype(jnp.float32)
-        ).astype(jnp.bfloat16)
+    spans = [slice(at, at + tile) for at in range(0, out_ref.shape[1], tile)]
+
+    def product(span):
+        return jnp.dot(hidden, cot_ref[:, span], preferred_element_type=jnp.float32).astype(
+            jnp.bfloat16
+        )
+
+    coming = product(spans[0])
+    for i, span in enumerate(spans):
+        gradient = coming
+        if i + 1 < len(spans):
+            coming = product(spans[i + 1])
+        out_ref[:, span] = adam_step(gradient, first_ref[:, span], second_ref[:, span])
 
 
 def update(hid_all, cot_whole, first_moment, second_moment):
     units, features = first_moment.shape
     groups, _, rows = hid_all.shape
-    tall = 256
+    tall = 384
     block = pl.BlockSpec((tall, features), lambda i: (i, 0))
     return pl.pallas_call(
         functools.partial(update_kernel, 512 if features % 512 == 0 else 128),

time: 95.4 us -> 87.2 us (0.914)
  Pallas kernels: 90.1 us -> 82.7 us
    pallas_call x1, Pallas kernels: 37.7 us -> 33.2 us  [update(): pl.pallas_call(functools.partial(update_kernel, 512 if features % 512 ==...]
    pallas_call x1, Pallas kernels: 52.5 us -> 49.5 us  [exchange(): pl.pallas_call(functools.partial(exchange_kernel, chunks, pieces, block),...]
  transfers between devices with their start and end apart: 1 -> 1, of which waited for: 0 -> 0; matrix products, arithmetic and copies ran while one was open for 0% -> 0% of each run, Pallas kernels for 40% -> 38%
where the time goes in v2:
time: 87.2 us; the launch traced here: 87.1 us
  Pallas kernels  82.7 us (95%)
  other arithmetic  2.8 us (3%)
  starting transfers between devices  0.92 us (1%)
    pallas_call x1, Pallas kernels, exchange(): pl.pallas_call(functools.partial(exchange_kernel, chunks, pieces, block),...  49.5 us
    pallas_call x1, Pallas kernels, update(): pl.pallas_call(functools.partial(update_kernel, 512 if features % 512 ==...  33.2 us
    convert_element_type x1, other arithmetic, shards(): (hidden_grad * gelu_slopes(pre_act.astype(jnp.float32))).astype(jnp.bfloa...  2.8 us
  transfers between devices with their start and end apart: 1, of which 0 were waited for; matrix products, arithmetic and copies ran while one was open for 0% of the time, Pallas kernels for 38%

profile of v2, /device:TPU:0, one launch (start us, length us, event | category | flops | bytes accessed | tf_op | source)
XLA Modules:
  0.0 87.1 jit_solution(6208914396889722393)
XLA Ops:
  0.6 49.5 %exchange.1 = (bf16[8,64,2560]{2,1,0:T(8,128)(2,1)}, bf16[4,4608,128]{2,1,0:T(8,128)(2,1)}, bf16[128,4608]{1,0:T(8,128)(2,1)}, bf16[128,4608]{1,0:T(8,128)(2,1)}) custom-call(bf16[128,4608]{1,0:T(8,128)(2,1)} %pre_ref.1, bf16[64,2560]{1,0:T(8,128)(2,1)} %cot_ref.1, bf16[4608,2560]{1,0:T(8,128)(2,1)} %weight_ref.1), custom_call_target="tpu_custom_call" | custom-call | tf_op jit(solution)/shard_map/exchange/pallas_call | solution.py:269
  50.1 0.9 %collective-permute-start = (bf16[128,4608]{1,0:T(8,128)(2,1)}, bf16[128,4608]{1,0:T(8,128)(2,1)S(1)}, u32[]{:S(2)}, u32[]{:S(2)}) collective-permute-start(bf16[128,4608]{1,0:T(8,128)(2,1)} %get-tuple-element.7), channel_id=1, source_target_pairs={{0,2},{1,3},{2,0},{3,1},{4,6},{5,7},{6,4},{7,5},{8,10},{9,11},{10,... | collective-permute-start | bytes 3538952 | tf_op jit(solution)/shard_map/ppermute | solution.py:348
  51.1 0.0 copy-start
  51.1 0.0 copy-start.1
  51.1 33.2 %update.1 = bf16[4608,2560]{1,0:T(8,128)(2,1)} custom-call(bf16[4,4608,128]{2,1,0:T(8,128)(2,1)} %get-tuple-element.8.hid_ref, bf16[512,2560]{1,0:T(8,128)(2,1)} %bitcast.1, bf16[4608,2560]{1,0:T(8,128)(2,1)} %first_ref.1, bf16[4608,2560]{1,0:T(8,128)(2,1)} %second_ref.1), custom_call_target="tpu_custom_call" | custom-call | flops 12079595520 | bytes 70778880 | tf_op jit(solution)/shard_map/update/pallas_call | solution.py:325
  84.3 0.0 collective-permute-done
  84.3 0.0 copy-done
  84.3 0.0 copy-done.1
  84.3 2.8 %fusion.7 = bf16[128,4608]{1,0:T(8,128)(2,1)} fusion(bf16[128,4608]{1,0:T(8,128)(2,1)S(1)} %copy-done, bf16[128,4608]{1,0:T(8,128)(2,1)S(1)} %collective-permute-done, bf16[128,4608]{1,0:T(8,128)(2,1)S(1)} %copy-done.1), kind=kLoop, calls=%fused_computation.14 | loop fusion | flops 13565952 | bytes 4718592 | tf_op jit(solution)/shard_map/convert_element_type | solution.py:352
Async XLA Ops:
  50.1 34.1 %collective-permute-start = (bf16[128,4608]{1,0:T(8,128)(2,1)}, bf16[128,4608]{1,0:T(8,128)(2,1)S(1)}, u32[]{:S(2)}, u32[]{:S(2)}) collective-permute-start(bf16[128,4608]{1,0:T(8,128)(2,1)} %get-tuple-element.7), channel_id=1, source_target_pairs={{0,2},{1,3},{2,0},{3,1},{4,6},{5,7},{6,4},{7,5},{8,10},{9,11},{10,... | collective-permute-start | bytes 3538952 | tf_op jit(solution)/shard_map/ppermute | solution.py:348
  51.1 33.2 %copy-start = (bf16[128,4608]{1,0:T(8,128)(2,1)S(1)}, bf16[128,4608]{1,0:T(8,128)(2,1)}, u32[]{:S(2)}) copy-start(bf16[128,4608]{1,0:T(8,128)(2,1)} %pre_ref.1) | copy-start | bytes 3538948
  51.1 33.2 %copy-start.1 = (bf16[128,4608]{1,0:T(8,128)(2,1)S(1)}, bf16[128,4608]{1,0:T(8,128)(2,1)}, u32[]{:S(2)}) copy-start(bf16[128,4608]{1,0:T(8,128)(2,1)} %get-tuple-element.6) | copy-start | bytes 3538948

commit v3 on v2

--- a/solution.py
+++ b/solution.py
@@ -43,10 +43,10 @@
 def exchange_kernel(
     chunks, pieces, block,
     pre_ref, cot_ref, weight_ref,
-    cot_all, hid_all, mine_ref, away_ref,
-    weight, hidden, total, part, other,
+    cot_out, hid_all, mine_ref, away_ref,
+    weight, hidden, total, part, other, turned, cot_all,
     weight_sem, own_sem, ring_send, ring_recv, hid_send, hid_recv, fwd_send, fwd_recv,
-    pair_send, pair_recv,
+    pair_send, pair_recv, out_sem,
 ):
     mp, dp = lax.axis_index("mp"), lax.axis_index("dp")
     tokens, features = cot_ref.shape
@@ -172,25 +172,29 @@
         hid_begin(ahead)
 
     def multiply(k, first, last):
+        copy = pltpu.make_async_copy(
+            cot_all.at[:, :, columns(k)], cot_out.at[:, :, columns(k)], out_sem.at[k]
+        )
+        copy.start()
+        kept.append(copy)
         loads[k].wait()
-        cot = cot_all[:, :, k * wide : (k + 1) * wide].reshape(8 * tokens, wide)
+        turned[...] = cot_all[:, :, k * wide : (k + 1) * wide].reshape(8 * tokens, wide).T
 
         span = block if last else 2 * block
 
         def one(i, carry):
             at = pl.ds(pl.multiple_of(i * span, span), span)
-            product = lax.dot_general(
-                cot,
-                weight[at, columns(k)],
-                (((1,), (1,)), ((), ())),
-                preferred_element_type=jnp.float32,
+            product = jnp.dot(
+                weight[at, columns(k)], turned[...], preferred_element_type=jnp.float32
             )
             if not first:
-                product = product + total[:, at]
+                product = product + total[at, :]
             if not last:
-                total[:, at] = product
+                total[at, :] = product
                 return carry
-            part[:, :, at] = product.astype(jnp.bfloat16).reshape(4, rows, block)
+            rounded = product.astype(jnp.bfloat16)
+            for owner in range(4):
+                part[owner, at, :] = rounded[:, owner * rows : (owner + 1) * rows]
             for side in (0, 1):
                 pair_copy(i, side).start()
             return carry
@@ -200,8 +204,8 @@
     def pair_copy(i, side):
         at = pl.ds(pl.multiple_of(i * block, block), block)
         return pltpu.make_async_remote_copy(
-            src_ref=part.at[2 * side + 1 - core, :, at],
-            dst_ref=other.at[side, :, at],
+            src_ref=part.at[2 * side + 1 - core, at, :],
+            dst_ref=other.at[side, at, :],
             send_sem=pair_send.at[i, side],
             recv_sem=pair_recv.at[i, side],
             device_id={"dp": sibling},
@@ -239,12 +243,11 @@
         at = pl.ds(pl.multiple_of(i * block, block), block)
         for side in (0, 1):
             pair_copy(i, side).wait()
-        mine = part[2 * y + core, :, at].astype(jnp.float32) + other[y, :, at].astype(jnp.float32)
-        away = part[2 * (1 - y) + core, :, at].astype(jnp.float32) + other[1 - y, :, at].astype(
-            jnp.float32
-        )
-        mine_ref[:, at] = mine.astype(jnp.bfloat16)
-        away_ref[:, at] = away.astype(jnp.bfloat16)
+        for owner, out_ref in ((y, mine_ref), (1 - y, away_ref)):
+            summed = part[2 * owner + core, at, :].astype(jnp.float32) + other[
+                owner, at, :
+            ].astype(jnp.float32)
+            out_ref[:, at] = summed.T.astype(jnp.bfloat16)
         return carry
 
     lax.fori_loop(0, units // block, combine, 0)
@@ -275,13 +278,15 @@
             jax.ShapeDtypeStruct((rows, units), bf16),
         ),
         in_specs=[vmem, vmem, hbm],
-        out_specs=(vmem, hbm, vmem, vmem),
+        out_specs=(hbm, hbm, vmem, vmem),
         scratch_shapes=[
             pltpu.VMEM((units, features), bf16),
             pltpu.VMEM((units, rows), bf16),
-            pltpu.VMEM((8 * tokens, units), jnp.float32),
-            pltpu.VMEM((4, rows, units), bf16),
-            pltpu.VMEM((2, rows, units), bf16),
+            pltpu.VMEM((units, 8 * tokens), jnp.float32),
+            pltpu.VMEM((4, units, rows), bf16),
+            pltpu.VMEM((2, units, rows), bf16),
+            pltpu.VMEM((features // chunks, 8 * tokens), bf16),
+            pltpu.VMEM((8, tokens, features), bf16),
             dma((chunks,)),
             dma((pieces,)),
             dma((chunks, 4, 2)),
@@ -292,6 +297,7 @@
             dma((pieces,)),
             dma((units // block, 2)),
             dma((units // block, 2)),
+            dma((chunks,)),
         ],
         compiler_params=pltpu.CompilerParams(
             collective_id=0, has_side_effects=True, vmem_limit_bytes=60 * 2**20
@@ -320,7 +326,7 @@
 def update(hid_all, cot_whole, first_moment, second_moment):
     units, features = first_moment.shape
     groups, _, rows = hid_all.shape
-    tall = 384
+    tall = 512 if units % 512 == 0 else 384
     block = pl.BlockSpec((tall, features), lambda i: (i, 0))
     return pl.pallas_call(
         functools.partial(update_kernel, 512 if features % 512 == 0 else 128),

time: 87.2 us -> 86.9 us (level)
    pallas_call x1, Pallas kernels: 49.5 us -> 48.6 us  [exchange(): pl.pallas_call(functools.partial(exchange_kernel, chunks, pieces, block),...]
  transfers between devices with their start and end apart: 1 -> 1, of which waited for: 0 -> 0; matrix products, arithmetic and copies ran while one was open for 0% -> 0% of each run, Pallas kernels for 38% -> 39%
where the time goes in v3:
time: 86.9 us; the launch traced here: 86.8 us
  Pallas kernels  82.5 us (95%)
  other arithmetic  2.8 us (3%)
    pallas_call x1, Pallas kernels, exchange(): pl.pallas_call(functools.partial(exchange_kernel, chunks, pieces, block),...  48.6 us
    pallas_call x1, Pallas kernels, update(): pl.pallas_call(functools.partial(update_kernel, 512 if features % 512 ==...  33.9 us
    convert_element_type x1, other arithmetic, shards(): (hidden_grad * gelu_slopes(pre_act.astype(jnp.float32))).astype(jnp.bfloa...  2.8 us
  transfers between devices with their start and end apart: 1, of which 0 were waited for; matrix products, arithmetic and copies ran while one was open for 0% of the time, Pallas kernels for 39%

profile of v3, /device:TPU:0, one launch (start us, length us, event | category | flops | bytes accessed | tf_op | source)
XLA Modules:
  0.0 86.8 jit_solution(3520797518804281752)
XLA Ops:
  0.6 48.6 %exchange.1 = (bf16[8,64,2560]{2,1,0:T(8,128)(2,1)}, bf16[4,4608,128]{2,1,0:T(8,128)(2,1)}, bf16[128,4608]{1,0:T(8,128)(2,1)}, bf16[128,4608]{1,0:T(8,128)(2,1)}) custom-call(bf16[128,4608]{1,0:T(8,128)(2,1)} %pre_ref.1, bf16[64,2560]{1,0:T(8,128)(2,1)} %cot_ref.1, bf16[4608,2560]{1,0:T(8,128)(2,1)} %weight_ref.1), custom_call_target="tpu_custom_call" | custom-call | tf_op jit(solution)/shard_map/exchange/pallas_call | solution.py:272
  49.3 0.8 collective-permute-start
  50.1 0.0 copy-start
  50.1 0.0 copy-start.1
  50.1 33.9 %update.1 = bf16[4608,2560]{1,0:T(8,128)(2,1)} custom-call(bf16[4,4608,128]{2,1,0:T(8,128)(2,1)} %get-tuple-element.8.hid_ref, bf16[512,2560]{1,0:T(8,128)(2,1)} %bitcast.1, bf16[4608,2560]{1,0:T(8,128)(2,1)} %first_ref.1, bf16[4608,2560]{1,0:T(8,128)(2,1)} %second_ref.1), custom_call_target="tpu_custom_call" | custom-call | flops 12079595520 | bytes 70778880 | tf_op jit(solution)/shard_map/update/pallas_call | solution.py:331
  84.0 0.0 collective-permute-done
  84.0 0.0 copy-done
  84.0 0.0 copy-done.1
  84.0 2.8 %fusion.7 = bf16[128,4608]{1,0:T(8,128)(2,1)} fusion(bf16[128,4608]{1,0:T(8,128)(2,1)S(1)} %copy-done, bf16[128,4608]{1,0:T(8,128)(2,1)S(1)} %collective-permute-done, bf16[128,4608]{1,0:T(8,128)(2,1)S(1)} %copy-done.1), kind=kLoop, calls=%fused_computation.14 | loop fusion | flops 13565952 | bytes 4718592 | tf_op jit(solution)/shard_map/convert_element_type | solution.py:358
Async XLA Ops:
  49.3 34.7 %collective-permute-start = (bf16[128,4608]{1,0:T(8,128)(2,1)}, bf16[128,4608]{1,0:T(8,128)(2,1)S(1)}, u32[]{:S(2)}, u32[]{:S(2)}) collective-permute-start(bf16[128,4608]{1,0:T(8,128)(2,1)} %get-tuple-element.7), channel_id=1, source_target_pairs={{0,2},{1,3},{2,0},{3,1},{4,6},{5,7},{6,4},{7,5},{8,10},{9,11},{10,... | collective-permute-start | bytes 3538952 | tf_op jit(solution)/shard_map/ppermute | solution.py:354
  50.1 33.9 %copy-start = (bf16[128,4608]{1,0:T(8,128)(2,1)S(1)}, bf16[128,4608]{1,0:T(8,128)(2,1)}, u32[]{:S(2)}) copy-start(bf16[128,4608]{1,0:T(8,128)(2,1)} %pre_ref.1) | copy-start | bytes 3538948
  50.1 33.9 %copy-start.1 = (bf16[128,4608]{1,0:T(8,128)(2,1)S(1)}, bf16[128,4608]{1,0:T(8,128)(2,1)}, u32[]{:S(2)}) copy-start(bf16[128,4608]{1,0:T(8,128)(2,1)} %get-tuple-element.6) | copy-start | bytes 3538948
